TPU v7x, 512 devices: a whole 4x4x16 slice. The times are simulated.
512 devices in a mesh: lat: 32 (over z_lo, x), lon: 16 (over y, z_hi, core).
Axes of the slice: x: 4, y: 4, z: 16 (z_hi: 2, z_lo: 8; z = z_hi * 8 + z_lo), core: 2. Of those that a mesh axis runs over, the one named last changes fastest.
Arguments:
- grid_field: bfloat16 [512, 2880, 64], P('lat', 'lon'), may hold values from -6 to 6
- disco_reach: int32 [512], P('lat'), may hold values from 1 to 20, as said below
- disco_taps: float32 [512, 492], P('lat'), may hold values from -1 to 1
- disco_weight: bfloat16 [4, 64, 64], replicated, may hold values from -0.375 to 0.375
- legendre: bfloat16 [512, 32, 768], P('lat', 'lon'), may hold values from -0.25 to 0.25
- spectral_mixing_weight: bfloat16 [768, 2, 64, 64], P('lat'), may hold values from -0.5 to 0.5
Outputs:
- block_out: bfloat16 [512, 2880, 64], P('lat', 'lon')
Inputs may be any that keep to these rules, and one draw needn't show every extreme that they name: `disco_reach`: the rows at both poles reach 20.
All inputs are finite; a program needn't handle non-finite values.
Results may differ from a plain program's by a relative error of at most 0.02.
Values may be sent and summed in bfloat16 or wider, within the bound.
No kernel may reach another device: no remote copies, remote signals or barrier semaphores. Data moves between devices by JAX's collectives and lax.ppermute only.
A program may use at most 128 MiB of HBM per device.

v0:
```python
import math
import jax
import jax.numpy as jnp
from jax import lax
from jax.sharding import PartitionSpec as P

NLON = 2880
HMAX = 20
BASES = 4


def padded(cells, sides, width, closed):
    for axis, dim in sides:
        count = lax.axis_size(axis)
        ends = count if closed else count - 1
        head = lax.slice_in_dim(cells, 0, width, axis=dim)
        tail = lax.slice_in_dim(cells, cells.shape[dim] - width, cells.shape[dim], axis=dim)
        cells = jnp.concatenate(
            [
                lax.ppermute(tail, axis, [(i, (i + 1) % count) for i in range(ends)]),
                cells,
                lax.ppermute(head, axis, [((i + 1) % count, i) for i in range(ends)]),
            ],
            axis=dim,
        )
    return cells


def angles(columns, orders):
    residues = columns[:, None] * orders[None, :] % NLON
    return residues.astype(jnp.float32) * (2.0 * math.pi / NLON)


def forward_table(columns, orders):
    phases = angles(columns, orders)
    factor = 1.0 / math.sqrt(NLON)
    return jnp.stack([jnp.cos(phases) * factor, -jnp.sin(phases) * factor], axis=1).astype(
        jnp.bfloat16
    )


def inverse_table(orders, columns, mode_count):
    phases = angles(columns, orders)
    factor = 1.0 / math.sqrt(mode_count)
    return jnp.stack([jnp.cos(phases).T * factor, -jnp.sin(phases).T * factor], axis=0).astype(
        jnp.bfloat16
    )


def disco(grid_field, disco_reach, disco_taps, disco_weight):
    lat_rows, lon_cols, channels = grid_field.shape
    tap_count = 2 * HMAX + 1
    widened = padded(grid_field, (("lon", 1),), HMAX, True)
    extended = padded(widened, (("lat", 0),), 1, False)
    flattened = extended.reshape(lat_rows + 2, (lon_cols + 2 * HMAX) * channels)
    offsets = jnp.abs(jnp.arange(tap_count, dtype=jnp.int32) - HMAX)
    within = offsets[None, :] <= disco_reach[:, None]
    kernel_coef = jnp.where(
        within[:, None, None, :], disco_taps.reshape(lat_rows, BASES, 3, tap_count), 0.0
    )
    running_totals = [
        jnp.zeros((lat_rows, lon_cols * channels), jnp.float32) for kernel in range(BASES)
    ]
    for lat_step in range(3):
        for lon_step in range(tap_count):
            window = flattened[
                lat_step : lat_step + lat_rows,
                lon_step * channels : (lon_step + lon_cols) * channels,
            ].astype(jnp.float32)
            for kernel in range(BASES):
                running_totals[kernel] = (
                    running_totals[kernel]
                    + kernel_coef[:, kernel, lat_step, lon_step][:, None] * window
                )
    basis_sums = (
        jnp.stack(running_totals, axis=1)
        .astype(jnp.bfloat16)
        .reshape(lat_rows, BASES, lon_cols, channels)
    )
    return jnp.einsum("rkjc,kcd->rjd", basis_sums, disco_weight, preferred_element_type=jnp.float32)


def per_device(grid_field, disco_reach, disco_taps, disco_weight, legendre, spectral_mixing_weight):
    lat_rows, lon_cols, channels = grid_field.shape
    orders_dev = legendre.shape[1]
    lon_count = lax.axis_size("lon")
    lat_count = lax.axis_size("lat")
    mode_count = orders_dev * lon_count
    harmonic_degree_rows = legendre.shape[2] // lat_count
    lon_place = lax.axis_index("lon")
    disco_out = disco(grid_field, disco_reach, disco_taps, disco_weight)
    mode_index = jnp.arange(mode_count, dtype=jnp.int32)
    own_columns = lon_place * lon_cols + jnp.arange(lon_cols, dtype=jnp.int32)
    full_table = forward_table(jnp.arange(NLON, dtype=jnp.int32), mode_index)
    row_spectra = jnp.einsum(
        "blv,lis->bsiv",
        lax.all_to_all(grid_field, "lon", split_axis=0, concat_axis=1, tiled=True),
        full_table,
        preferred_element_type=jnp.float32,
    ).astype(jnp.bfloat16)
    spectra = lax.all_to_all(row_spectra, "lon", split_axis=1, concat_axis=0, tiled=True).reshape(
        lat_rows, orders_dev, 2 * channels
    )
    orders_global = lon_place * orders_dev + jnp.arange(orders_dev, dtype=jnp.int32)

    def masked(amount):
        degree = jnp.arange(amount, dtype=jnp.int32)
        within = degree[None, :] >= orders_global[:, None]
        return jnp.where(within[None], legendre, jnp.zeros((), jnp.bfloat16))

    coeffs = lax.psum_scatter(
        jnp.einsum(
            "iml,imc->lmc",
            masked(harmonic_degree_rows * lax.axis_size("lat")),
            spectra,
            preferred_element_type=jnp.float32,
        ).astype(jnp.bfloat16),
        "lat",
        scatter_dimension=0,
        tiled=True,
    )
    real_part = spectral_mixing_weight[:, 0]
    imag_part = spectral_mixing_weight[:, 1]
    upper = jnp.concatenate([real_part, imag_part], axis=2)
    lower = jnp.concatenate([-imag_part, real_part], axis=2)
    complex_block = jnp.concatenate([upper, lower], axis=1)
    mixed_modes = jnp.einsum(
        "lmc,lcd->lmd", coeffs, complex_block, preferred_element_type=jnp.float32
    ).astype(jnp.bfloat16)
    portion = lax.all_gather(mixed_modes, "lat", axis=0, tiled=True)
    grid_modes = jnp.einsum(
        "iml,lmc->imc", masked(portion.shape[0]), portion, preferred_element_type=jnp.float32
    ).astype(jnp.bfloat16)
    own_inverse = inverse_table(mode_index, own_columns, mode_count)
    portion = lax.all_gather(grid_modes, "lon", axis=1, tiled=True)
    amount = portion.shape[1]
    shaped = portion.reshape(lat_rows, amount, 2, channels)
    spectral_out = jnp.einsum(
        "impc,pmj->ijc", shaped, own_inverse, preferred_element_type=jnp.float32
    ).astype(jnp.bfloat16)
    combined = spectral_out.astype(jnp.float32) + disco_out
    return (grid_field.astype(jnp.float32) + jax.nn.gelu(combined, approximate=True)).astype(
        jnp.bfloat16
    )


def solution(mesh):
    in_specs = (
        P("lat", "lon", None),
        P("lat"),
        P("lat", None),
        P(),
        P("lat", "lon", None),
        P("lat", None, None, None),
    )
    out_specs = P("lat", "lon", None)
    return jax.shard_map(
        per_device, mesh=mesh, in_specs=in_specs, out_specs=out_specs, check_vma=False
    )
```

profile of v0, /device:TPU:1, one launch (start us, length us, event | category | flops | bytes accessed | tf_op | source)
XLA Modules:
  0.0 830.0 jit_solution(7017814243375401134)
XLA Ops:
  6.5 19.4 %all-to-all-start = ((bf16[16,180,64]{1,2,0:T(8,128)(2,1)}), bf16[16,180,64]{1,2,0:T(8,128)(2,1)S(1)}, u32[]{:S(2)}, u32[]{:S(2)}) async-start(bf16[16,180,64]{1,2,0:T(8,128)(2,1)} %param.6), calls=%async_computation | async-start | bytes 1048576 | tf_op jit(solution)/shard_map/all_to_all | solution.py:97
  25.9 0.9 fusion.562
  26.8 12.2 %collective-permute-start = (bf16[16,20,64]{1,2,0:T(8,128)(2,1)}, bf16[16,20,64]{1,2,0:T(8,128)(2,1)S(1)}, u32[]{:S(2)}, u32[]{:S(2)}) collective-permute-start(bf16[16,20,64]{1,2,0:T(8,128)(2,1)} %get-tuple-element.501), channel_id=1, source_target_pairs={{0,1},{1,2},{2,3},{3,4},{4,5},{5,6},{6,7},{7,8},{8,9},{9,10},{10,1... | collective-permute-start | bytes 122888 | tf_op jit(solution)/shard_map/ppermute | solution.py:20
  39.0 1.9 collective-permute-start.1
  41.3 1.5 slice_reduce_fusion.486
  42.8 1.4 slice_reduce_fusion.491
  44.2 1.5 slice_reduce_fusion.490
  45.7 1.5 slice_reduce_fusion.489
  47.2 1.5 slice_reduce_fusion.488
  48.7 1.5 slice_reduce_fusion.487
  50.1 1.3 slice_reduce_fusion.485
  51.4 1.5 slice_reduce_fusion.363
  53.0 1.5 slice_reduce_fusion.362
  54.5 1.5 slice_reduce_fusion.361
  55.9 1.5 slice_reduce_fusion.360
  57.4 1.5 slice_reduce_fusion.359
  58.9 1.4 slice_reduce_fusion.358
  60.3 1.3 slice_reduce_fusion.357
  61.6 1.5 slice_reduce_fusion.235
  63.1 1.5 slice_reduce_fusion.234
  64.6 1.7 slice_reduce_fusion.233
  66.3 1.5 slice_reduce_fusion.232
  67.7 1.5 slice_reduce_fusion.231
  69.2 1.5 slice_reduce_fusion.230
  70.7 1.5 slice_reduce_fusion.107
  72.2 1.5 slice_reduce_fusion.106
  73.6 1.5 slice_reduce_fusion.105
  75.1 1.5 slice_reduce_fusion.104
  76.6 1.5 slice_reduce_fusion.103
  78.1 2.3 multiply_convert_fusion
  80.4 1.0 slice_bitcast_fusion
  81.4 0.8 fusion.561
  82.5 1.3 slice_reduce_fusion.229
  83.9 3.1 collective-permute-start.2
  87.0 1.7 collective-permute-start.3
  88.7 1.3 slice_reduce_fusion.102
  90.0 1.3 dynamic-slice
  91.9 0.4 pad_maximum_fusion
  92.3 0.7 copy.66
  93.2 0.9 reshape.742
  94.5 32.1 %fusion.533 = bf16[16,11520]{1,0:T(8,128)(2,1)S(1)} fusion(f32[16]{0:T(128)S(1)} %copy-done.117, f32[16]{0:T(128)S(1)} %copy-done.118, f32[16]{0:T(128)S(1)} %copy-done.119, f32[16]{0:T(128)S(1)} %copy-done.120, f32[16]{0:T(128)S(1)} %copy-done.121, f32[16]{0:T(128)S(1)} %copy-done.122, f32[16]{0:T(128)S(1)} %copy-done.123, f32[16]{0:T(128)S(1)} %copy-done.124, ...), kind=kLoop, calls=%fused_computation.1021 | loop fusion | flops 68014080 | bytes 45719232 | tf_op jit(solution)/shard_map/convert.8
  126.7 33.0 %fusion.532 = bf16[16,11520]{1,0:T(8,128)(2,1)} fusion(f32[16]{0:T(128)S(1)} %copy-done.89, f32[16]{0:T(128)S(1)} %copy-done.90, f32[16]{0:T(128)S(1)} %copy-done.91, f32[16]{0:T(128)S(1)} %copy-done.92, f32[16]{0:T(128)S(1)} %copy-done.93, f32[16]{0:T(128)S(1)} %copy-done.94, f32[16]{0:T(128)S(1)} %copy-done.95, f32[16]{0:T(128)S(1)} %copy-done.96, ...), kind=kLoop, calls=%fused_computation.1020 | loop fusion | flops 68014080 | bytes 45719232 | tf_op jit(solution)/shard_map/convert.7
  160.5 0.7 reshape.743
  161.2 1.3 fusion.18
  162.5 0.7 reshape.1243
  163.2 15.7 %all-to-all-start.1 = ((bf16[16,2,128]{2,1,0:T(2,128)(2,1)}), bf16[16,2,128]{2,1,0:T(2,128)(2,1)S(1)}, u32[]{:S(2)}, u32[]{:S(2)}) async-start(bf16[16,2,128]{2,1,0:T(2,128)(2,1)} %reshape.1243), calls=%async_computation.1 | async-start | bytes 16384 | tf_op jit(solution)/shard_map/all_to_all | solution.py:101
  179.4 31.8 %fusion.531 = bf16[16,11520]{1,0:T(8,128)(2,1)S(1)} fusion(f32[16]{0:T(128)S(1)} %copy-done.50, f32[16]{0:T(128)S(1)} %copy-done.51, f32[16]{0:T(128)S(1)} %copy-done.52, f32[16]{0:T(128)S(1)} %copy-done.54, f32[16]{0:T(128)S(1)} %copy-done.55, f32[16]{0:T(128)S(1)} %copy-done.56, f32[16]{0:T(128)S(1)} %copy-done.57, f32[16]{0:T(128)S(1)} %copy-done.58, ...), kind=kLoop, calls=%fused_computation.1019 | loop fusion | flops 68014080 | bytes 45719232 | tf_op jit(solution)/shard_map/convert.6
  211.8 0.3 fusion.17
  212.1 1.1 copy.59
  213.6 31.9 %fusion.530 = bf16[16,11520]{1,0:T(8,128)(2,1)S(1)} fusion(f32[16]{0:T(128)S(1)} %copy-done.10, f32[16]{0:T(128)S(1)} %copy-done.11, f32[16]{0:T(128)S(1)} %copy-done.12, f32[16]{0:T(128)S(1)} %copy-done.13, f32[16]{0:T(128)S(1)} %copy-done.14, f32[16]{0:T(128)S(1)} %copy-done.15, f32[16]{0:T(128)S(1)} %copy-done.16, f32[16]{0:T(128)S(1)} %copy-done.17, ...), kind=kLoop, calls=%fused_computation.1018 | loop fusion | flops 68014080 | bytes 45719232 | tf_op jit(solution)/shard_map/convert.5
  245.4 0.5 stack.29
  245.9 0.3 copy.67
  246.4 0.5 stack.30
  246.9 1.2 copy.68
  248.1 0.5 stack.31
  248.6 1.1 copy.69
  249.7 0.5 stack.32
  250.2 1.1 copy.70
  251.3 384.7 %all-reduce.3.cloned.1.call-done = bf16[768,2,128]{2,1,0:T(2,128)(2,1)} async-done(((bf16[768,2,128]{2,1,0:T(2,128)(2,1)}), bf16[768,2,128]{2,1,0:T(2,128)(2,1)}) %all-reduce.3.cloned.1.call-update) | async-done | bytes 393232
  636.1 1.7 convolution_convert_fusion.2
  637.7 107.0 %all_gather.6 = bf16[768,2,128]{2,1,0:T(2,128)(2,1)S(1)} all-gather(bf16[24,2,128]{2,1,0:T(2,128)(2,1)S(1)} %convolution_convert_fusion.2), channel_id=1, replica_groups=mesh['lat'=32,'lon'=16] {'lat'}, dimensions={0}, use_global_device_ids=true | all-gather | bytes 405504 | tf_op jit(solution)/shard_map/all_gather | solution.py:130
  744.9 74.4 %all_gather.7 = bf16[16,32,128]{2,0,1:T(8,128)(2,1)S(1)} all-gather(bf16[16,2,128]{2,0,1:T(8,128)(2,1)S(1)} %fusion.19), channel_id=1, replica_groups=mesh['lat'=32,'lon'=16] {'lon'}, dimensions={1}, use_global_device_ids=true | all-gather | bytes 139264 | tf_op jit(solution)/shard_map/all_gather | solution.py:135
  819.4 0.4 fusion.16
  819.8 2.9 fusion.32
  (280 shorter events, 2.2 us)
Async XLA Ops:
  6.5 813.2 %copy-start = (bf16[4,64,64]{2,1,0:T(8,128)(2,1)S(1)}, bf16[4,64,64]{2,1,0:T(8,128)(2,1)}, u32[]{:S(2)}) copy-start(bf16[4,64,64]{2,1,0:T(8,128)(2,1)} %param.9) | copy-start | bytes 98308
  6.5 19.4 %copy-start.1 = (bf16[16,180,64]{1,2,0:T(8,128)(2,1)S(1)}, bf16[16,180,64]{1,2,0:T(8,128)(2,1)}, u32[]{:S(2)}) copy-start(bf16[16,180,64]{1,2,0:T(8,128)(2,1)} %param.6) | copy-start | bytes 1105924
  6.5 34.4 %copy-start.9 = (f32[16,492]{1,0:T(8,128)S(1)}, f32[16,492]{1,0:T(8,128)}, u32[]{:S(2)}) copy-start(f32[16,492]{1,0:T(8,128)} %param.8) | copy-start | bytes 94468
  6.5 34.6 %copy-start.127 = (s32[16]{0:T(128)S(1)}, s32[16]{0:T(128)}, u32[]{:S(2)}) copy-start(s32[16]{0:T(128)} %param.7) | copy-start | bytes 196
  6.5 153.2 %all-to-all-start = ((bf16[16,180,64]{1,2,0:T(8,128)(2,1)}), bf16[16,180,64]{1,2,0:T(8,128)(2,1)S(1)}, u32[]{:S(2)}, u32[]{:S(2)}) async-start(bf16[16,180,64]{1,2,0:T(8,128)(2,1)} %param.6), calls=%async_computation | async-start | bytes 1048576 | tf_op jit(solution)/shard_map/all_to_all | solution.py:97
  26.8 57.0 %collective-permute-start = (bf16[16,20,64]{1,2,0:T(8,128)(2,1)}, bf16[16,20,64]{1,2,0:T(8,128)(2,1)S(1)}, u32[]{:S(2)}, u32[]{:S(2)}) collective-permute-start(bf16[16,20,64]{1,2,0:T(8,128)(2,1)} %get-tuple-element.501), channel_id=1, source_target_pairs={{0,1},{1,2},{2,3},{3,4},{4,5},{5,6},{6,7},{7,8},{8,9},{9,10},{10,1... | collective-permute-start | bytes 122888 | tf_op jit(solution)/shard_map/ppermute | solution.py:20
  39.0 44.7 %collective-permute-start.1 = (bf16[16,20,64]{1,2,0:T(8,128)(2,1)S(1)}, bf16[16,20,64]{1,2,0:T(8,128)(2,1)S(1)}, u32[]{:S(2)}, u32[]{:S(2)}) collective-permute-start(bf16[16,20,64]{1,2,0:T(8,128)(2,1)S(1)} %get-tuple-element.502), channel_id=1, source_target_pairs={{1,0},{2,1},{3,2},{4,3},{5,4},{6,5},{7,6},{8,7},{9,8},{10,9},{11,1... | collective-permute-start | bytes 122888 | tf_op jit(solution)/shard_map/ppermute | solution.py:22
  83.9 8.0 collective-permute-start.2
  87.0 4.9 collective-permute-start.3
  94.4 32.2 %copy-start.88 = (f32[16]{0:T(128)S(1)}, f32[16]{0:T(128)}, u32[]{:S(2)}) copy-start(f32[16]{0:T(128)} %get-tuple-element.133) | copy-start | bytes 196
  94.4 32.2 %copy-start.89 = (f32[16]{0:T(128)S(1)}, f32[16]{0:T(128)}, u32[]{:S(2)}) copy-start(f32[16]{0:T(128)} %get-tuple-element.144) | copy-start | bytes 196
  94.4 32.2 %copy-start.90 = (f32[16]{0:T(128)S(1)}, f32[16]{0:T(128)}, u32[]{:S(2)}) copy-start(f32[16]{0:T(128)} %get-tuple-element.145) | copy-start | bytes 196
  94.5 32.2 %copy-start.91 = (f32[16]{0:T(128)S(1)}, f32[16]{0:T(128)}, u32[]{:S(2)}) copy-start(f32[16]{0:T(128)} %get-tuple-element.146) | copy-start | bytes 196
  94.5 32.2 %copy-start.92 = (f32[16]{0:T(128)S(1)}, f32[16]{0:T(128)}, u32[]{:S(2)}) copy-start(f32[16]{0:T(128)} %get-tuple-element.147) | copy-start | bytes 196
  94.5 32.2 %copy-start.93 = (f32[16]{0:T(128)S(1)}, f32[16]{0:T(128)}, u32[]{:S(2)}) copy-start(f32[16]{0:T(128)} %get-tuple-element.148) | copy-start | bytes 196
  94.5 32.2 %copy-start.94 = (f32[16]{0:T(128)S(1)}, f32[16]{0:T(128)}, u32[]{:S(2)}) copy-start(f32[16]{0:T(128)} %get-tuple-element.149) | copy-start | bytes 196
  94.5 32.2 %copy-start.95 = (f32[16]{0:T(128)S(1)}, f32[16]{0:T(128)}, u32[]{:S(2)}) copy-start(f32[16]{0:T(128)} %get-tuple-element.150) | copy-start | bytes 196
  94.5 32.2 %copy-start.96 = (f32[16]{0:T(128)S(1)}, f32[16]{0:T(128)}, u32[]{:S(2)}) copy-start(f32[16]{0:T(128)} %get-tuple-element.151) | copy-start | bytes 196
  94.5 32.2 %copy-start.126 = (f32[16]{0:T(128)S(1)}, f32[16]{0:T(128)}, u32[]{:S(2)}) copy-start(f32[16]{0:T(128)} %get-tuple-element.152) | copy-start | bytes 196
  160.1 18.9 %copy-start.49 = (f32[16]{0:T(128)S(1)}, f32[16]{0:T(128)}, u32[]{:S(2)}) copy-start(f32[16]{0:T(128)} %get-tuple-element.261) | copy-start | bytes 196
  160.1 18.9 %copy-start.50 = (f32[16]{0:T(128)S(1)}, f32[16]{0:T(128)}, u32[]{:S(2)}) copy-start(f32[16]{0:T(128)} %get-tuple-element.277) | copy-start | bytes 196
  160.1 18.9 %copy-start.51 = (f32[16]{0:T(128)S(1)}, f32[16]{0:T(128)}, u32[]{:S(2)}) copy-start(f32[16]{0:T(128)} %get-tuple-element.278) | copy-start | bytes 196
  160.1 18.9 %copy-start.52 = (f32[16]{0:T(128)S(1)}, f32[16]{0:T(128)}, u32[]{:S(2)}) copy-start(f32[16]{0:T(128)} %get-tuple-element.279) | copy-start | bytes 196
  160.1 18.9 %copy-start.53 = (f32[16]{0:T(128)S(1)}, f32[16]{0:T(128)}, u32[]{:S(2)}) copy-start(f32[16]{0:T(128)} %get-tuple-element.280) | copy-start | bytes 196
  160.2 18.9 %copy-start.54 = (f32[16]{0:T(128)S(1)}, f32[16]{0:T(128)}, u32[]{:S(2)}) copy-start(f32[16]{0:T(128)} %get-tuple-element.281) | copy-start | bytes 196
  160.2 18.9 %copy-start.55 = (f32[16]{0:T(128)S(1)}, f32[16]{0:T(128)}, u32[]{:S(2)}) copy-start(f32[16]{0:T(128)} %get-tuple-element.282) | copy-start | bytes 196
  160.2 18.9 %copy-start.56 = (f32[16]{0:T(128)S(1)}, f32[16]{0:T(128)}, u32[]{:S(2)}) copy-start(f32[16]{0:T(128)} %get-tuple-element.283) | copy-start | bytes 196
  160.2 18.9 %copy-start.57 = (f32[16]{0:T(128)S(1)}, f32[16]{0:T(128)}, u32[]{:S(2)}) copy-start(f32[16]{0:T(128)} %get-tuple-element.284) | copy-start | bytes 196
  160.2 18.9 %copy-start.58 = (f32[16]{0:T(128)S(1)}, f32[16]{0:T(128)}, u32[]{:S(2)}) copy-start(f32[16]{0:T(128)} %get-tuple-element.285) | copy-start | bytes 196
  160.2 18.9 %copy-start.59 = (f32[16]{0:T(128)S(1)}, f32[16]{0:T(128)}, u32[]{:S(2)}) copy-start(f32[16]{0:T(128)} %get-tuple-element.286) | copy-start | bytes 196
  160.2 18.9 %copy-start.60 = (f32[16]{0:T(128)S(1)}, f32[16]{0:T(128)}, u32[]{:S(2)}) copy-start(f32[16]{0:T(128)} %get-tuple-element.287) | copy-start | bytes 196
  160.2 18.9 %copy-start.61 = (f32[16]{0:T(128)S(1)}, f32[16]{0:T(128)}, u32[]{:S(2)}) copy-start(f32[16]{0:T(128)} %get-tuple-element.288) | copy-start | bytes 196
  160.2 18.9 %copy-start.62 = (f32[16]{0:T(128)S(1)}, f32[16]{0:T(128)}, u32[]{:S(2)}) copy-start(f32[16]{0:T(128)} %get-tuple-element.289) | copy-start | bytes 196
  160.2 18.9 %copy-start.63 = (f32[16]{0:T(128)S(1)}, f32[16]{0:T(128)}, u32[]{:S(2)}) copy-start(f32[16]{0:T(128)} %get-tuple-element.290) | copy-start | bytes 196
  160.3 18.9 %copy-start.64 = (f32[16]{0:T(128)S(1)}, f32[16]{0:T(128)}, u32[]{:S(2)}) copy-start(f32[16]{0:T(128)} %get-tuple-element.291) | copy-start | bytes 196
  160.3 18.9 %copy-start.65 = (f32[16]{0:T(128)S(1)}, f32[16]{0:T(128)}, u32[]{:S(2)}) copy-start(f32[16]{0:T(128)} %get-tuple-element.292) | copy-start | bytes 196
  160.3 18.9 %copy-start.66 = (f32[16]{0:T(128)S(1)}, f32[16]{0:T(128)}, u32[]{:S(2)}) copy-start(f32[16]{0:T(128)} %get-tuple-element.293) | copy-start | bytes 196
  160.3 18.9 %copy-start.67 = (f32[16]{0:T(128)S(1)}, f32[16]{0:T(128)}, u32[]{:S(2)}) copy-start(f32[16]{0:T(128)} %get-tuple-element.294) | copy-start | bytes 196
  160.3 18.9 %copy-start.68 = (f32[16]{0:T(128)S(1)}, f32[16]{0:T(128)}, u32[]{:S(2)}) copy-start(f32[16]{0:T(128)} %get-tuple-element.295) | copy-start | bytes 196
  160.3 18.9 %copy-start.69 = (f32[16]{0:T(128)S(1)}, f32[16]{0:T(128)}, u32[]{:S(2)}) copy-start(f32[16]{0:T(128)} %get-tuple-element.296) | copy-start | bytes 196
  160.3 18.9 %copy-start.70 = (f32[16]{0:T(128)S(1)}, f32[16]{0:T(128)}, u32[]{:S(2)}) copy-start(f32[16]{0:T(128)} %get-tuple-element.297) | copy-start | bytes 196
  160.3 18.9 %copy-start.71 = (f32[16]{0:T(128)S(1)}, f32[16]{0:T(128)}, u32[]{:S(2)}) copy-start(f32[16]{0:T(128)} %get-tuple-element.298) | copy-start | bytes 196
  160.3 18.9 %copy-start.72 = (f32[16]{0:T(128)S(1)}, f32[16]{0:T(128)}, u32[]{:S(2)}) copy-start(f32[16]{0:T(128)} %get-tuple-element.299) | copy-start | bytes 196
  160.3 18.9 %copy-start.73 = (f32[16]{0:T(128)S(1)}, f32[16]{0:T(128)}, u32[]{:S(2)}) copy-start(f32[16]{0:T(128)} %get-tuple-element.300) | copy-start | bytes 196
  160.4 18.9 %copy-start.74 = (f32[16]{0:T(128)S(1)}, f32[16]{0:T(128)}, u32[]{:S(2)}) copy-start(f32[16]{0:T(128)} %get-tuple-element.301) | copy-start | bytes 196
  160.4 18.9 %copy-start.75 = (f32[16]{0:T(128)S(1)}, f32[16]{0:T(128)}, u32[]{:S(2)}) copy-start(f32[16]{0:T(128)} %get-tuple-element.302) | copy-start | bytes 196
  160.4 18.9 %copy-start.76 = (f32[16]{0:T(128)S(1)}, f32[16]{0:T(128)}, u32[]{:S(2)}) copy-start(f32[16]{0:T(128)} %get-tuple-element.303) | copy-start | bytes 196
  160.4 18.9 %copy-start.77 = (f32[16]{0:T(128)S(1)}, f32[16]{0:T(128)}, u32[]{:S(2)}) copy-start(f32[16]{0:T(128)} %get-tuple-element.304) | copy-start | bytes 196
  160.4 18.9 %copy-start.78 = (f32[16]{0:T(128)S(1)}, f32[16]{0:T(128)}, u32[]{:S(2)}) copy-start(f32[16]{0:T(128)} %get-tuple-element.305) | copy-start | bytes 196
  160.4 18.9 %copy-start.79 = (f32[16]{0:T(128)S(1)}, f32[16]{0:T(128)}, u32[]{:S(2)}) copy-start(f32[16]{0:T(128)} %get-tuple-element.306) | copy-start | bytes 196
  160.4 18.9 %copy-start.80 = (f32[16]{0:T(128)S(1)}, f32[16]{0:T(128)}, u32[]{:S(2)}) copy-start(f32[16]{0:T(128)} %get-tuple-element.307) | copy-start | bytes 196
  160.4 18.9 %copy-start.81 = (f32[16]{0:T(128)S(1)}, f32[16]{0:T(128)}, u32[]{:S(2)}) copy-start(f32[16]{0:T(128)} %get-tuple-element.308) | copy-start | bytes 196
  160.4 18.9 %copy-start.82 = (f32[16]{0:T(128)S(1)}, f32[16]{0:T(128)}, u32[]{:S(2)}) copy-start(f32[16]{0:T(128)} %get-tuple-element.309) | copy-start | bytes 196
  160.4 18.9 %copy-start.83 = (f32[16]{0:T(128)S(1)}, f32[16]{0:T(128)}, u32[]{:S(2)}) copy-start(f32[16]{0:T(128)} %get-tuple-element.310) | copy-start | bytes 196
  160.5 18.9 %copy-start.84 = (f32[16]{0:T(128)S(1)}, f32[16]{0:T(128)}, u32[]{:S(2)}) copy-start(f32[16]{0:T(128)} %get-tuple-element.311) | copy-start | bytes 196
  160.5 18.9 %copy-start.85 = (f32[16]{0:T(128)S(1)}, f32[16]{0:T(128)}, u32[]{:S(2)}) copy-start(f32[16]{0:T(128)} %get-tuple-element.312) | copy-start | bytes 196
  160.5 18.9 %copy-start.86 = (f32[16]{0:T(128)S(1)}, f32[16]{0:T(128)}, u32[]{:S(2)}) copy-start(f32[16]{0:T(128)} %get-tuple-element.313) | copy-start | bytes 196
  160.5 18.9 %copy-start.87 = (f32[16]{0:T(128)S(1)}, f32[16]{0:T(128)}, u32[]{:S(2)}) copy-start(f32[16]{0:T(128)} %get-tuple-element.314) | copy-start | bytes 196
  163.2 48.4 %all-to-all-start.1 = ((bf16[16,2,128]{2,1,0:T(2,128)(2,1)}), bf16[16,2,128]{2,1,0:T(2,128)(2,1)S(1)}, u32[]{:S(2)}, u32[]{:S(2)}) async-start(bf16[16,2,128]{2,1,0:T(2,128)(2,1)} %reshape.1243), calls=%async_computation.1 | async-start | bytes 16384 | tf_op jit(solution)/shard_map/all_to_all | solution.py:101
  178.9 457.2 %all-reduce.3.cloned.1.call-start = ((), (), s32[]{:S(2)}) async-start(), calls=%async_computation.2 | async-start | bytes 786432
  249.7 386.4 %copy-start.6 = (bf16[24,64,64]{2,1,0:T(8,128)(2,1)S(1)}, bf16[24,64,64]{2,1,0:T(8,128)(2,1)}, u32[]{:S(2)}) copy-start(bf16[24,64,64]{2,1,0:T(8,128)(2,1)} %fusion.561) | copy-start | bytes 589828
  250.2 385.9 %copy-start.7 = (bf16[24,64,64]{2,1,0:T(8,128)(2,1)S(1)}, bf16[24,64,64]{2,1,0:T(8,128)(2,1)}, u32[]{:S(2)}) copy-start(bf16[24,64,64]{2,1,0:T(8,128)(2,1)} %get-tuple-element.499) | copy-start | bytes 589828
  744.9 74.9 %copy-start.4 = (bf16[16,1,180,64]{2,3,1,0:T(8,128)(2,1)S(1)}, bf16[16,1,180,64]{2,3,1,0:T(8,128)(2,1)}, u32[]{:S(2)}) copy-start(bf16[16,1,180,64]{2,3,1,0:T(8,128)(2,1)} %copy.68) | copy-start | bytes 1105924
  744.9 74.9 %copy-start.5 = (bf16[16,1,180,64]{2,3,1,0:T(8,128)(2,1)S(1)}, bf16[16,1,180,64]{2,3,1,0:T(8,128)(2,1)}, u32[]{:S(2)}) copy-start(bf16[16,1,180,64]{2,3,1,0:T(8,128)(2,1)} %copy.69) | copy-start | bytes 1105924
  (71 other events, 132.4 us)
Sparse Core Ops, SparseCore 0:
  213.3 422.7 all-reduce.2
where the time goes:
time: 839 us; the launch traced here: 830 us
  waiting for transfers between devices  385 us (46%)
  blocking collectives  181 us (22%)
  other arithmetic  133 us (16%)
  starting transfers between devices  54.1 us (6%)
  local copies, waits for them, and re-layouts  53.6 us (6%)
  between operations  16.6 us (2%)
    unnamed x2, waiting for transfers between devices  385 us
    another operation x6, other arithmetic  131 us
    all_gather x1, blocking collectives, per_device(): portion = lax.all_gather(mixed_modes, 'lat', axis=0, tiled=True)  107 us
    all_gather x1, blocking collectives, per_device(): portion = lax.all_gather(grid_modes, 'lon', axis=1, tiled=True)  74.4 us
    slice x27, local copies, waits for them, and re-layouts, disco(): kernel_coef[:, kernel, lat_step, lon_step][:, None] * window  39.3 us
    all_to_all x1, starting transfers between devices, per_device(): lax.all_to_all(grid_field, 'lon', split_axis=0, concat_axis=1, tiled=True)  19.4 us
  transfers between devices with their start and end apart: 7, of which 1 were waited for; matrix products, arithmetic and copies ran while one was open for 22% of the time, Pallas kernels for 0%

commit v1 on v0

--- a/solution.py
+++ b/solution.py
@@ -127,7 +127,8 @@
     mixed_modes = jnp.einsum(
         "lmc,lcd->lmd", coeffs, complex_block, preferred_element_type=jnp.float32
     ).astype(jnp.bfloat16)
-    portion = lax.all_gather(mixed_modes, "lat", axis=0, tiled=True)
+    outgoing = jnp.stack([mixed_modes] * lax.axis_size("lat"))
+    portion = jnp.concatenate(lax.all_to_all(outgoing, "lat", 0, 0), axis=0)
     grid_modes = jnp.einsum(
         "iml,lmc->imc", masked(portion.shape[0]), portion, preferred_element_type=jnp.float32
     ).astype(jnp.bfloat16)

time: 839 us -> 731 us (0.87)
  blocking collectives: 181 us -> 61 us
  starting transfers between devices: 54.1 us -> 63.8 us
    all_gather x1 -> x0, blocking collectives: 107 us -> none  [per_device(): portion = lax.all_gather(mixed_modes, 'lat', axis=0, tiled=True)]
    all_gather x1, blocking collectives: 74.4 us -> 61 us  [per_device(): portion = lax.all_gather(grid_modes, 'lon', axis=1, tiled=True)]
    all_to_all x0 -> x1, starting transfers between devices: none -> 9.51 us  [per_device(): portion = jnp.concatenate(lax.all_to_all(outgoing, 'lat', 0, 0), axis=0)]
  transfers between devices with their start and end apart: 7 -> 8, of which waited for: 1 -> 1; matrix products, arithmetic and copies ran while one was open for 22% -> 25% of each run, Pallas kernels for 0% -> 0%
where the time goes in v1:
time: 731 us; the launch traced here: 721 us
  waiting for transfers between devices  387 us (53%)
  other arithmetic  132 us (18%)
  starting transfers between devices  63.8 us (9%)
  blocking collectives  61 us (8%)
  local copies, waits for them, and re-layouts  54.5 us (7%)
  between operations  17.2 us (2%)
    unnamed x2, waiting for transfers between devices  387 us
    another operation x6, other arithmetic  130 us
    all_gather x1, blocking collectives, per_device(): portion = lax.all_gather(grid_modes, 'lon', axis=1, tiled=True)  61 us
    slice x27, local copies, waits for them, and re-layouts, disco(): kernel_coef[:, kernel, lat_step, lon_step][:, None] * window  39.3 us
    all_to_all x1, starting transfers between devices, per_device(): lax.all_to_all(grid_field, 'lon', split_axis=0, concat_axis=1, tiled=True)  19.4 us
    all_to_all x1, starting transfers between devices, per_device(): lax.all_to_all(row_spectra, 'lon', split_axis=1, concat_axis=0, tiled=True)  15.7 us
    ppermute x2, starting transfers between devices, padded(): lax.ppermute(tail, axis, [(i, (i + 1) % count) for i in range(ends)])  15.4 us
  transfers between devices with their start and end apart: 8, of which 1 were waited for; matrix products, arithmetic and copies ran while one was open for 25% of the time, Pallas kernels for 0%

profile of v1, /device:TPU:1, one launch (start us, length us, event | category | flops | bytes accessed | tf_op | source)
XLA Modules:
  0.0 721.5 jit_solution(82374373181835394)
XLA Ops:
  6.5 19.4 %all-to-all-start = ((bf16[16,180,64]{1,2,0:T(8,128)(2,1)}), bf16[16,180,64]{1,2,0:T(8,128)(2,1)S(1)}, u32[]{:S(2)}, u32[]{:S(2)}) async-start(bf16[16,180,64]{1,2,0:T(8,128)(2,1)} %param.6), calls=%async_computation | async-start | bytes 1048576 | tf_op jit(solution)/shard_map/all_to_all | solution.py:97
  25.9 0.9 fusion.561
  26.8 12.2 %collective-permute-start = (bf16[16,20,64]{1,2,0:T(8,128)(2,1)}, bf16[16,20,64]{1,2,0:T(8,128)(2,1)S(1)}, u32[]{:S(2)}, u32[]{:S(2)}) collective-permute-start(bf16[16,20,64]{1,2,0:T(8,128)(2,1)} %get-tuple-element.501), channel_id=1, source_target_pairs={{0,1},{1,2},{2,3},{3,4},{4,5},{5,6},{6,7},{7,8},{8,9},{9,10},{10,1... | collective-permute-start | bytes 122888 | tf_op jit(solution)/shard_map/ppermute | solution.py:20
  39.0 1.9 collective-permute-start.1
  41.3 1.5 slice_reduce_fusion.486
  42.8 1.4 slice_reduce_fusion.491
  44.2 1.5 slice_reduce_fusion.490
  45.7 1.5 slice_reduce_fusion.489
  47.2 1.5 slice_reduce_fusion.488
  48.7 1.5 slice_reduce_fusion.487
  50.1 1.3 slice_reduce_fusion.485
  51.4 1.5 slice_reduce_fusion.363
  53.0 1.5 slice_reduce_fusion.362
  54.4 1.5 slice_reduce_fusion.361
  55.9 1.5 slice_reduce_fusion.360
  57.4 1.5 slice_reduce_fusion.359
  58.9 1.4 slice_reduce_fusion.358
  60.3 1.3 slice_reduce_fusion.357
  61.6 1.5 slice_reduce_fusion.235
  63.1 1.5 slice_reduce_fusion.234
  64.6 1.7 slice_reduce_fusion.233
  66.3 1.5 slice_reduce_fusion.232
  67.7 1.5 slice_reduce_fusion.231
  69.2 1.5 slice_reduce_fusion.230
  70.7 1.5 slice_reduce_fusion.107
  72.2 1.5 slice_reduce_fusion.106
  73.7 1.5 slice_reduce_fusion.105
  75.1 1.5 slice_reduce_fusion.104
  76.6 1.5 slice_reduce_fusion.103
  78.1 2.3 multiply_convert_fusion
  80.4 1.0 slice_bitcast_fusion
  81.4 0.8 fusion.560
  82.5 1.3 slice_reduce_fusion.229
  83.9 3.1 collective-permute-start.2
  87.0 1.7 collective-permute-start.3
  88.7 1.3 slice_reduce_fusion.102
  90.0 1.3 dynamic-slice
  91.9 0.4 pad_maximum_fusion
  92.3 0.7 copy.72
  93.4 0.9 reshape.748
  94.6 32.2 %fusion.533 = bf16[16,11520]{1,0:T(8,128)(2,1)S(1)} fusion(f32[16]{0:T(128)S(1)} %copy-done.145, f32[16]{0:T(128)S(1)} %copy-done.146, f32[16]{0:T(128)S(1)} %copy-done.147, f32[16]{0:T(128)S(1)} %copy-done.148, f32[16]{0:T(128)S(1)} %copy-done.149, f32[16]{0:T(128)S(1)} %copy-done.150, f32[16]{0:T(128)S(1)} %copy-done.151, f32[16]{0:T(128)S(1)} %copy-done.152, ...), kind=kLoop, calls=%fused_computation.1021 | loop fusion | flops 68014080 | bytes 45719232 | tf_op jit(solution)/shard_map/convert.8
  127.5 0.7 reshape.749
  128.2 1.3 fusion.18
  129.5 0.7 reshape.1249
  130.2 15.7 %all-to-all-start.1 = ((bf16[16,2,128]{2,1,0:T(2,128)(2,1)}), bf16[16,2,128]{2,1,0:T(2,128)(2,1)S(1)}, u32[]{:S(2)}, u32[]{:S(2)}) async-start(bf16[16,2,128]{2,1,0:T(2,128)(2,1)} %reshape.1249), calls=%async_computation.1 | async-start | bytes 16384 | tf_op jit(solution)/shard_map/all_to_all | solution.py:101
  146.6 31.9 %fusion.532 = bf16[16,11520]{1,0:T(8,128)(2,1)S(1)} fusion(f32[16]{0:T(128)S(1)} %copy-done.87, f32[16]{0:T(128)S(1)} %copy-done.88, f32[16]{0:T(128)S(1)} %copy-done.89, f32[16]{0:T(128)S(1)} %copy-done.90, f32[16]{0:T(128)S(1)} %copy-done.91, f32[16]{0:T(128)S(1)} %copy-done.92, f32[16]{0:T(128)S(1)} %copy-done.93, f32[16]{0:T(128)S(1)} %copy-done.94, ...), kind=kLoop, calls=%fused_computation.1020 | loop fusion | flops 68014080 | bytes 45719232 | tf_op jit(solution)/shard_map/convert.7
  179.4 1.1 copy.64
  180.9 31.8 %fusion.531 = bf16[16,11520]{1,0:T(8,128)(2,1)S(1)} fusion(f32[16]{0:T(128)S(1)} %copy-done.48, f32[16]{0:T(128)S(1)} %copy-done.49, f32[16]{0:T(128)S(1)} %copy-done.50, f32[16]{0:T(128)S(1)} %copy-done.52, f32[16]{0:T(128)S(1)} %copy-done.53, f32[16]{0:T(128)S(1)} %copy-done.54, f32[16]{0:T(128)S(1)} %copy-done.55, f32[16]{0:T(128)S(1)} %copy-done.56, ...), kind=kLoop, calls=%fused_computation.1019 | loop fusion | flops 68014080 | bytes 45719232 | tf_op jit(solution)/shard_map/convert.6
  212.7 0.5 stack.21
  213.2 0.3 copy.73
  213.5 0.5 stack.22
  214.0 1.1 copy.74
  215.2 0.5 stack.23
  215.7 1.1 copy.75
  216.8 386.6 %all-reduce.3.cloned.1.call-done = bf16[768,2,128]{2,1,0:T(2,128)(2,1)} async-done(((bf16[768,2,128]{2,1,0:T(2,128)(2,1)}), bf16[768,2,128]{2,1,0:T(2,128)(2,1)}) %all-reduce.3.cloned.1.call-update) | async-done | bytes 393232
  603.4 1.8 convolution_convert_fusion.2
  605.5 0.8 stack.20
  606.3 9.5 %all-to-all-start.2 = ((bf16[32,24,2,128]{3,1,2,0:T(8,128)(2,1)}), bf16[32,24,2,128]{3,1,2,0:T(8,128)(2,1)S(1)}, u32[]{:S(2)}, u32[]{:S(2)}) async-start(bf16[32,24,2,128]{3,1,2,0:T(8,128)(2,1)} %stack.20), calls=%async_computation.2 | async-start | bytes 786432 | tf_op jit(solution)/shard_map/all_to_all | solution.py:131
  616.2 31.6 %fusion.530 = bf16[16,11520]{1,0:T(8,128)(2,1)S(1)} fusion(f32[16]{0:T(128)S(1)} %copy-done.8, f32[16]{0:T(128)S(1)} %copy-done.9, f32[16]{0:T(128)S(1)} %copy-done.10, f32[16]{0:T(128)S(1)} %copy-done.11, f32[16]{0:T(128)S(1)} %copy-done.12, f32[16]{0:T(128)S(1)} %copy-done.13, f32[16]{0:T(128)S(1)} %copy-done.14, f32[16]{0:T(128)S(1)} %copy-done.15, ...), kind=kLoop, calls=%fused_computation.1018 | loop fusion | flops 68014080 | bytes 45719232 | tf_op jit(solution)/shard_map/convert.5
  647.8 0.5 stack.24
  648.3 1.2 copy.76
  649.7 61.0 %all_gather.3 = bf16[16,32,128]{2,0,1:T(8,128)(2,1)S(1)} all-gather(bf16[16,2,128]{2,0,1:T(8,128)(2,1)S(1)} %fusion.19), channel_id=1, replica_groups=mesh['lat'=32,'lon'=16] {'lon'}, dimensions={1}, use_global_device_ids=true | all-gather | bytes 139264 | tf_op jit(solution)/shard_map/all_gather | solution.py:136
  710.9 0.4 fusion.16
  711.3 2.9 fusion.32
  (356 shorter events, 2.7 us)
Async XLA Ops:
  6.5 704.7 %copy-start = (bf16[4,64,64]{2,1,0:T(8,128)(2,1)S(1)}, bf16[4,64,64]{2,1,0:T(8,128)(2,1)}, u32[]{:S(2)}) copy-start(bf16[4,64,64]{2,1,0:T(8,128)(2,1)} %param.9) | copy-start | bytes 98308
  6.5 19.4 %copy-start.1 = (bf16[16,180,64]{1,2,0:T(8,128)(2,1)S(1)}, bf16[16,180,64]{1,2,0:T(8,128)(2,1)}, u32[]{:S(2)}) copy-start(bf16[16,180,64]{1,2,0:T(8,128)(2,1)} %param.6) | copy-start | bytes 1105924
  6.5 34.4 %copy-start.7 = (f32[16,492]{1,0:T(8,128)S(1)}, f32[16,492]{1,0:T(8,128)}, u32[]{:S(2)}) copy-start(f32[16,492]{1,0:T(8,128)} %param.8) | copy-start | bytes 94468
  6.5 34.6 %copy-start.163 = (s32[16]{0:T(128)S(1)}, s32[16]{0:T(128)}, u32[]{:S(2)}) copy-start(s32[16]{0:T(128)} %param.7) | copy-start | bytes 196
  6.5 120.3 %all-to-all-start = ((bf16[16,180,64]{1,2,0:T(8,128)(2,1)}), bf16[16,180,64]{1,2,0:T(8,128)(2,1)S(1)}, u32[]{:S(2)}, u32[]{:S(2)}) async-start(bf16[16,180,64]{1,2,0:T(8,128)(2,1)} %param.6), calls=%async_computation | async-start | bytes 1048576 | tf_op jit(solution)/shard_map/all_to_all | solution.py:97
  26.8 57.0 %collective-permute-start = (bf16[16,20,64]{1,2,0:T(8,128)(2,1)}, bf16[16,20,64]{1,2,0:T(8,128)(2,1)S(1)}, u32[]{:S(2)}, u32[]{:S(2)}) collective-permute-start(bf16[16,20,64]{1,2,0:T(8,128)(2,1)} %get-tuple-element.501), channel_id=1, source_target_pairs={{0,1},{1,2},{2,3},{3,4},{4,5},{5,6},{6,7},{7,8},{8,9},{9,10},{10,1... | collective-permute-start | bytes 122888 | tf_op jit(solution)/shard_map/ppermute | solution.py:20
  39.0 44.8 %collective-permute-start.1 = (bf16[16,20,64]{1,2,0:T(8,128)(2,1)S(1)}, bf16[16,20,64]{1,2,0:T(8,128)(2,1)S(1)}, u32[]{:S(2)}, u32[]{:S(2)}) collective-permute-start(bf16[16,20,64]{1,2,0:T(8,128)(2,1)S(1)} %get-tuple-element.502), channel_id=1, source_target_pairs={{1,0},{2,1},{3,2},{4,3},{5,4},{6,5},{7,6},{8,7},{9,8},{10,9},{11,1... | collective-permute-start | bytes 122888 | tf_op jit(solution)/shard_map/ppermute | solution.py:22
  63.1 17.3 %copy-start.2 = (bf16[24,2,64,64]{3,2,1,0:T(8,128)(2,1)S(1)}, bf16[24,2,64,64]{3,2,1,0:T(8,128)(2,1)}, u32[]{:S(2)}) copy-start(bf16[24,2,64,64]{3,2,1,0:T(8,128)(2,1)} %param.11) | copy-start | bytes 1179652
  83.9 8.0 %collective-permute-start.2 = (bf16[1,220,64]{1,2,0:T(8,128)(2,1)S(1)}, bf16[1,220,64]{1,2,0:T(8,128)(2,1)S(1)}, u32[]{:S(2)}, u32[]{:S(2)}) collective-permute-start(bf16[1,220,64]{1,2,0:T(8,128)(2,1)S(1)} %get-tuple-element.497), channel_id=1, source_target_pairs={{0,16},{16,32},{32,48},{48,64},{64,80},{80,96},{96,112},{112,128},... | collective-permute-start | bytes 84488 | tf_op jit(solution)/shard_map/ppermute | solution.py:20
  87.0 4.9 collective-permute-start.3
  127.1 19.0 %copy-start.86 = (f32[16]{0:T(128)S(1)}, f32[16]{0:T(128)}, u32[]{:S(2)}) copy-start(f32[16]{0:T(128)} %get-tuple-element.133) | copy-start | bytes 196
  127.1 19.0 %copy-start.87 = (f32[16]{0:T(128)S(1)}, f32[16]{0:T(128)}, u32[]{:S(2)}) copy-start(f32[16]{0:T(128)} %get-tuple-element.144) | copy-start | bytes 196
  127.1 19.0 %copy-start.88 = (f32[16]{0:T(128)S(1)}, f32[16]{0:T(128)}, u32[]{:S(2)}) copy-start(f32[16]{0:T(128)} %get-tuple-element.145) | copy-start | bytes 196
  127.2 19.0 %copy-start.89 = (f32[16]{0:T(128)S(1)}, f32[16]{0:T(128)}, u32[]{:S(2)}) copy-start(f32[16]{0:T(128)} %get-tuple-element.146) | copy-start | bytes 196
  127.2 19.0 %copy-start.90 = (f32[16]{0:T(128)S(1)}, f32[16]{0:T(128)}, u32[]{:S(2)}) copy-start(f32[16]{0:T(128)} %get-tuple-element.147) | copy-start | bytes 196
  127.2 19.0 %copy-start.91 = (f32[16]{0:T(128)S(1)}, f32[16]{0:T(128)}, u32[]{:S(2)}) copy-start(f32[16]{0:T(128)} %get-tuple-element.148) | copy-start | bytes 196
  127.2 19.0 %copy-start.92 = (f32[16]{0:T(128)S(1)}, f32[16]{0:T(128)}, u32[]{:S(2)}) copy-start(f32[16]{0:T(128)} %get-tuple-element.149) | copy-start | bytes 196
  127.2 19.0 %copy-start.93 = (f32[16]{0:T(128)S(1)}, f32[16]{0:T(128)}, u32[]{:S(2)}) copy-start(f32[16]{0:T(128)} %get-tuple-element.150) | copy-start | bytes 196
  127.2 19.0 %copy-start.94 = (f32[16]{0:T(128)S(1)}, f32[16]{0:T(128)}, u32[]{:S(2)}) copy-start(f32[16]{0:T(128)} %get-tuple-element.151) | copy-start | bytes 196
  127.2 19.0 %copy-start.95 = (f32[16]{0:T(128)S(1)}, f32[16]{0:T(128)}, u32[]{:S(2)}) copy-start(f32[16]{0:T(128)} %get-tuple-element.152) | copy-start | bytes 196
  127.2 19.0 %copy-start.96 = (f32[16]{0:T(128)S(1)}, f32[16]{0:T(128)}, u32[]{:S(2)}) copy-start(f32[16]{0:T(128)} %get-tuple-element.153) | copy-start | bytes 196
  127.2 19.0 %copy-start.97 = (f32[16]{0:T(128)S(1)}, f32[16]{0:T(128)}, u32[]{:S(2)}) copy-start(f32[16]{0:T(128)} %get-tuple-element.154) | copy-start | bytes 196
  127.2 19.0 %copy-start.98 = (f32[16]{0:T(128)S(1)}, f32[16]{0:T(128)}, u32[]{:S(2)}) copy-start(f32[16]{0:T(128)} %get-tuple-element.155) | copy-start | bytes 196
  127.3 19.0 %copy-start.99 = (f32[16]{0:T(128)S(1)}, f32[16]{0:T(128)}, u32[]{:S(2)}) copy-start(f32[16]{0:T(128)} %get-tuple-element.156) | copy-start | bytes 196
  127.3 19.0 %copy-start.100 = (f32[16]{0:T(128)S(1)}, f32[16]{0:T(128)}, u32[]{:S(2)}) copy-start(f32[16]{0:T(128)} %get-tuple-element.157) | copy-start | bytes 196
  127.3 19.0 %copy-start.101 = (f32[16]{0:T(128)S(1)}, f32[16]{0:T(128)}, u32[]{:S(2)}) copy-start(f32[16]{0:T(128)} %get-tuple-element.158) | copy-start | bytes 196
  127.3 19.0 %copy-start.102 = (f32[16]{0:T(128)S(1)}, f32[16]{0:T(128)}, u32[]{:S(2)}) copy-start(f32[16]{0:T(128)} %get-tuple-element.159) | copy-start | bytes 196
  127.3 19.0 %copy-start.103 = (f32[16]{0:T(128)S(1)}, f32[16]{0:T(128)}, u32[]{:S(2)}) copy-start(f32[16]{0:T(128)} %get-tuple-element.160) | copy-start | bytes 196
  127.3 19.0 %copy-start.104 = (f32[16]{0:T(128)S(1)}, f32[16]{0:T(128)}, u32[]{:S(2)}) copy-start(f32[16]{0:T(128)} %get-tuple-element.161) | copy-start | bytes 196
  127.3 19.0 %copy-start.105 = (f32[16]{0:T(128)S(1)}, f32[16]{0:T(128)}, u32[]{:S(2)}) copy-start(f32[16]{0:T(128)} %get-tuple-element.162) | copy-start | bytes 196
  127.3 19.0 %copy-start.106 = (f32[16]{0:T(128)S(1)}, f32[16]{0:T(128)}, u32[]{:S(2)}) copy-start(f32[16]{0:T(128)} %get-tuple-element.163) | copy-start | bytes 196
  127.3 19.0 %copy-start.107 = (f32[16]{0:T(128)S(1)}, f32[16]{0:T(128)}, u32[]{:S(2)}) copy-start(f32[16]{0:T(128)} %get-tuple-element.164) | copy-start | bytes 196
  127.3 19.0 %copy-start.108 = (f32[16]{0:T(128)S(1)}, f32[16]{0:T(128)}, u32[]{:S(2)}) copy-start(f32[16]{0:T(128)} %get-tuple-element.165) | copy-start | bytes 196
  127.4 19.0 %copy-start.109 = (f32[16]{0:T(128)S(1)}, f32[16]{0:T(128)}, u32[]{:S(2)}) copy-start(f32[16]{0:T(128)} %get-tuple-element.166) | copy-start | bytes 196
  127.4 19.0 %copy-start.110 = (f32[16]{0:T(128)S(1)}, f32[16]{0:T(128)}, u32[]{:S(2)}) copy-start(f32[16]{0:T(128)} %get-tuple-element.167) | copy-start | bytes 196
  127.4 19.0 %copy-start.111 = (f32[16]{0:T(128)S(1)}, f32[16]{0:T(128)}, u32[]{:S(2)}) copy-start(f32[16]{0:T(128)} %get-tuple-element.168) | copy-start | bytes 196
  127.4 19.0 %copy-start.112 = (f32[16]{0:T(128)S(1)}, f32[16]{0:T(128)}, u32[]{:S(2)}) copy-start(f32[16]{0:T(128)} %get-tuple-element.169) | copy-start | bytes 196
  127.4 19.0 %copy-start.113 = (f32[16]{0:T(128)S(1)}, f32[16]{0:T(128)}, u32[]{:S(2)}) copy-start(f32[16]{0:T(128)} %get-tuple-element.170) | copy-start | bytes 196
  127.4 19.0 %copy-start.114 = (f32[16]{0:T(128)S(1)}, f32[16]{0:T(128)}, u32[]{:S(2)}) copy-start(f32[16]{0:T(128)} %get-tuple-element.171) | copy-start | bytes 196
  127.4 19.0 %copy-start.115 = (f32[16]{0:T(128)S(1)}, f32[16]{0:T(128)}, u32[]{:S(2)}) copy-start(f32[16]{0:T(128)} %get-tuple-element.172) | copy-start | bytes 196
  127.4 19.0 %copy-start.116 = (f32[16]{0:T(128)S(1)}, f32[16]{0:T(128)}, u32[]{:S(2)}) copy-start(f32[16]{0:T(128)} %get-tuple-element.173) | copy-start | bytes 196
  127.4 19.0 %copy-start.117 = (f32[16]{0:T(128)S(1)}, f32[16]{0:T(128)}, u32[]{:S(2)}) copy-start(f32[16]{0:T(128)} %get-tuple-element.174) | copy-start | bytes 196
  127.4 19.0 %copy-start.118 = (f32[16]{0:T(128)S(1)}, f32[16]{0:T(128)}, u32[]{:S(2)}) copy-start(f32[16]{0:T(128)} %get-tuple-element.175) | copy-start | bytes 196
  127.5 19.0 %copy-start.119 = (f32[16]{0:T(128)S(1)}, f32[16]{0:T(128)}, u32[]{:S(2)}) copy-start(f32[16]{0:T(128)} %get-tuple-element.176) | copy-start | bytes 196
  127.5 19.0 %copy-start.120 = (f32[16]{0:T(128)S(1)}, f32[16]{0:T(128)}, u32[]{:S(2)}) copy-start(f32[16]{0:T(128)} %get-tuple-element.177) | copy-start | bytes 196
  127.5 19.0 %copy-start.121 = (f32[16]{0:T(128)S(1)}, f32[16]{0:T(128)}, u32[]{:S(2)}) copy-start(f32[16]{0:T(128)} %get-tuple-element.178) | copy-start | bytes 196
  127.5 19.0 %copy-start.122 = (f32[16]{0:T(128)S(1)}, f32[16]{0:T(128)}, u32[]{:S(2)}) copy-start(f32[16]{0:T(128)} %get-tuple-element.179) | copy-start | bytes 196
  127.5 19.0 %copy-start.123 = (f32[16]{0:T(128)S(1)}, f32[16]{0:T(128)}, u32[]{:S(2)}) copy-start(f32[16]{0:T(128)} %get-tuple-element.180) | copy-start | bytes 196
  127.5 19.0 %copy-start.124 = (f32[16]{0:T(128)S(1)}, f32[16]{0:T(128)}, u32[]{:S(2)}) copy-start(f32[16]{0:T(128)} %get-tuple-element.181) | copy-start | bytes 196
  130.2 48.7 %all-to-all-start.1 = ((bf16[16,2,128]{2,1,0:T(2,128)(2,1)}), bf16[16,2,128]{2,1,0:T(2,128)(2,1)S(1)}, u32[]{:S(2)}, u32[]{:S(2)}) async-start(bf16[16,2,128]{2,1,0:T(2,128)(2,1)} %reshape.1249), calls=%async_computation.1 | async-start | bytes 16384 | tf_op jit(solution)/shard_map/all_to_all | solution.py:101
  145.9 457.4 %all-reduce.3.cloned.1.call-start = ((), (), s32[]{:S(2)}) async-start(), calls=%async_computation.3 | async-start | bytes 786432
  215.7 387.7 %copy-start.5 = (bf16[24,64,64]{2,1,0:T(8,128)(2,1)S(1)}, bf16[24,64,64]{2,1,0:T(8,128)(2,1)}, u32[]{:S(2)}) copy-start(bf16[24,64,64]{2,1,0:T(8,128)(2,1)} %fusion.560) | copy-start | bytes 589828
  605.2 10.7 %copy-start.11 = (f32[16]{0:T(128)S(1)}, f32[16]{0:T(128)}, u32[]{:S(2)}) copy-start(f32[16]{0:T(128)} %get-tuple-element.393) | copy-start | bytes 196
  605.2 10.7 %copy-start.12 = (f32[16]{0:T(128)S(1)}, f32[16]{0:T(128)}, u32[]{:S(2)}) copy-start(f32[16]{0:T(128)} %get-tuple-element.394) | copy-start | bytes 196
  605.2 10.7 %copy-start.13 = (f32[16]{0:T(128)S(1)}, f32[16]{0:T(128)}, u32[]{:S(2)}) copy-start(f32[16]{0:T(128)} %get-tuple-element.395) | copy-start | bytes 196
  605.2 10.7 %copy-start.14 = (f32[16]{0:T(128)S(1)}, f32[16]{0:T(128)}, u32[]{:S(2)}) copy-start(f32[16]{0:T(128)} %get-tuple-element.396) | copy-start | bytes 196
  605.2 10.7 %copy-start.15 = (f32[16]{0:T(128)S(1)}, f32[16]{0:T(128)}, u32[]{:S(2)}) copy-start(f32[16]{0:T(128)} %get-tuple-element.397) | copy-start | bytes 196
  605.2 10.7 %copy-start.16 = (f32[16]{0:T(128)S(1)}, f32[16]{0:T(128)}, u32[]{:S(2)}) copy-start(f32[16]{0:T(128)} %get-tuple-element.398) | copy-start | bytes 196
  605.2 10.7 %copy-start.17 = (f32[16]{0:T(128)S(1)}, f32[16]{0:T(128)}, u32[]{:S(2)}) copy-start(f32[16]{0:T(128)} %get-tuple-element.399) | copy-start | bytes 196
  605.2 10.7 %copy-start.18 = (f32[16]{0:T(128)S(1)}, f32[16]{0:T(128)}, u32[]{:S(2)}) copy-start(f32[16]{0:T(128)} %get-tuple-element.400) | copy-start | bytes 196
  605.2 10.7 %copy-start.19 = (f32[16]{0:T(128)S(1)}, f32[16]{0:T(128)}, u32[]{:S(2)}) copy-start(f32[16]{0:T(128)} %get-tuple-element.401) | copy-start | bytes 196
  606.3 43.2 %all-to-all-start.2 = ((bf16[32,24,2,128]{3,1,2,0:T(8,128)(2,1)}), bf16[32,24,2,128]{3,1,2,0:T(8,128)(2,1)S(1)}, u32[]{:S(2)}, u32[]{:S(2)}) async-start(bf16[32,24,2,128]{3,1,2,0:T(8,128)(2,1)} %stack.20), calls=%async_computation.2 | async-start | bytes 786432 | tf_op jit(solution)/shard_map/all_to_all | solution.py:131
  649.7 61.6 %copy-start.3 = (bf16[16,1,180,64]{2,3,1,0:T(8,128)(2,1)S(1)}, bf16[16,1,180,64]{2,3,1,0:T(8,128)(2,1)}, u32[]{:S(2)}) copy-start(bf16[16,1,180,64]{2,3,1,0:T(8,128)(2,1)} %copy.74) | copy-start | bytes 1105924
  649.7 61.6 %copy-start.4 = (bf16[16,1,180,64]{2,3,1,0:T(8,128)(2,1)S(1)}, bf16[16,1,180,64]{2,3,1,0:T(8,128)(2,1)}, u32[]{:S(2)}) copy-start(bf16[16,1,180,64]{2,3,1,0:T(8,128)(2,1)} %copy.75) | copy-start | bytes 1105924
  (108 other events, 449.7 us)
Sparse Core Ops, SparseCore 0:
  180.6 422.7 all-reduce.2
